TPU v7x, 32 devices: a whole 2x2x4 slice. The times are simulated.
32 devices in a mesh: seq: 16 (over z, y, core), fsdp: 2 (over x).
Axes of the slice: x: 2, y: 2, z: 4, core: 2. Of those that a mesh axis runs over, the one named last changes fastest.
Arguments:
- tokens: float32 [1, 6144, 3072], P(None, 'seq', 'fsdp'), may hold values from -6 to 6
- block_mask: int32 [8, 6, 6], replicated, may hold values from 0 to 1, as said below
- space_qkv: bfloat16 [3072, 3, 512], P(None, None, 'fsdp'), may hold values from -0.109375 to 0.109375
- space_out: bfloat16 [512, 3072], P('fsdp'), may hold values from -0.375 to 0.375
- space_mod: float32 [3, 3072], replicated, may hold values from -2 to 3
- time_qkv: bfloat16 [3072, 3, 512], P(None, None, 'fsdp'), may hold values from -0.109375 to 0.109375
- time_out: bfloat16 [512, 3072], P('fsdp'), may hold values from -0.375 to 0.375
- time_mod: float32 [3, 3072], replicated, may hold values from -2 to 3
Outputs:
- result: float32 [1, 6144, 3072], P(None, 'seq', 'fsdp')
Inputs may be any that keep to these rules, and one draw needn't show every extreme that they name: block_mask[f, i, i] = 1 for every frame f and block i.
All inputs are finite; a program needn't handle non-finite values.
Results may differ from a plain program's by a relative error of at most 0.015.
Values may be sent and summed in bfloat16 or wider, within the bound.
A program may use at most 128 MiB of HBM per device.

v0:
```python
import functools
import math

import jax
import jax.numpy as jnp
from jax import lax
from jax.experimental import pallas as pl
from jax.experimental.pallas import tpu as pltpu
from jax.sharding import PartitionSpec as P

HD = 128
BLOCK = 128
EPS = 1e-06
RING = 8
STEPS = 4
MESH = pl.DeviceIdType.MESH
NT = (((1,), (1,)), ((), ()))


def softmax_rounded(scores):
    row_max = jnp.max(scores, axis=1, keepdims=True)
    lifted = jnp.exp(scores - row_max)
    return (lifted * (1.0 / jnp.sum(lifted, axis=1, keepdims=True))).astype(jnp.bfloat16)


def sublayers(
    sizes,
    mask_ref, tokens_ref, space_qkv_ref, space_out_ref, space_mod_ref, time_qkv_ref, time_out_ref,
    time_mod_ref, result_ref,
    stream, cols, total, queries, keys_values, mixed, sent_qkv, got_qkv, sent_att,
    space_w, cross_w, out_w, mods, stats, normed, h_time, part_sent, part_got, att_space, att_time,
    in_sem, w_sem, x_sem, o_sem, m_sem, out_sem,
    stat_s, stat_r, h_s, h_r, p_s, p_r, kv_s, kv_r, as_s, as_r, at_s, at_r,
    wq_s, wq_r, wf_s, wf_r, wc_s, wc_r, tq_s, tq_r, ta_s, ta_r,
):
    frames, parts, rows, part_width, heads_width, chunk = sizes
    chunks = rows // chunk
    piece = rows // frames
    per_chunk = chunk // piece
    step_rows = rows // STEPS
    per_step = step_rows // piece
    query_blocks = rows // BLOCK
    local_heads = heads_width // HD
    width = part_width * parts
    slab = part_width // RING
    lane_count = heads_width // 2
    scale = 1.0 / math.sqrt(HD)

    seq = lax.axis_index("seq")
    me = lax.axis_index("fsdp")
    half = lax.rem(seq, 2)
    frame = seq // 2
    place = lax.rem(frame, RING)
    base = frame - place

    def peer(distance):
        return lax.rem(me + distance, parts)

    def source(distance):
        return lax.rem(me + parts - distance, parts)

    def fsdp_copy(src, dst, send, recv, distance):
        return pltpu.make_async_remote_copy(
            src_ref=src, dst_ref=dst, send_sem=send, recv_sem=recv,
            device_id={"fsdp": peer(distance)}, device_id_type=MESH,
        )

    def seq_copy(src, dst, send, recv, target):
        return pltpu.make_async_remote_copy(
            src_ref=src, dst_ref=dst, send_sem=send, recv_sem=recv,
            device_id={"seq": target}, device_id_type=MESH,
        )

    out_refs = (space_out_ref, time_out_ref)
    mod_refs = (space_mod_ref, time_mod_ref)
    own_columns = pl.ds(pl.multiple_of(me * part_width, 128), part_width)
    other_core = seq + 1 - 2 * half

    def load_tokens():
        return pltpu.make_async_copy(tokens_ref.at[0], stream, in_sem)

    def load_space(kind):
        lanes = pl.ds(kind * heads_width, heads_width)
        return pltpu.make_async_copy(
            space_qkv_ref.at[kind], space_w.at[:, lanes], w_sem.at[kind]
        )

    def load_time():
        return pltpu.make_async_copy(
            time_qkv_ref.at[:, own_columns], cross_w.at[me], x_sem
        )

    def load_out(layer):
        return pltpu.make_async_copy(
            out_refs[layer].at[:, :, :, own_columns], out_w.at[layer, me], o_sem.at[layer]
        )

    def load_mod(layer):
        return pltpu.make_async_copy(
            mod_refs[layer].at[:, own_columns], mods.at[layer], m_sem.at[layer]
        )

    load_tokens().start()
    for layer in range(2):
        load_mod(layer).start()
    for kind in range(3):
        load_space(kind).start()

    barrier = pltpu.get_barrier_semaphore()
    for distance in range(1, parts):
        pl.semaphore_signal(barrier, inc=1, device_id={"fsdp": peer(distance)}, device_id_type=MESH)
    for distance in range(1, frames):
        other = lax.rem(frame + distance, frames) * 2 + half
        pl.semaphore_signal(barrier, inc=1, device_id={"seq": other}, device_id_type=MESH)
    pl.semaphore_signal(barrier, inc=1, device_id={"seq": other_core}, device_id_type=MESH)
    pl.semaphore_wait(barrier, parts + frames - 1)

    def slab_rows(first):
        return pl.ds(pl.multiple_of(first, 16), slab)

    own_lanes = pl.ds(pl.multiple_of(half * lane_count, 128), lane_count)

    def weight_piece(kind, owner, index):
        if kind == 1:
            return cross_w.at[owner, :, slab_rows(index * slab), own_lanes]
        return out_w.at[kind // 2, owner, index, half]

    def weight_copy(kind, distance):
        target = peer(distance)
        if kind == 1:
            first = target * part_width + place * slab
            block = time_qkv_ref.at[:, slab_rows(first), own_lanes]
        else:
            columns = pl.ds(pl.multiple_of(target * part_width, 128), part_width)
            block = out_refs[kind // 2].at[place, half, :, columns]
        return fsdp_copy(
            block, weight_piece(kind, me, place),
            wq_s.at[kind, distance], wq_r.at[kind, distance], distance,
        )

    def ring_copy(kind, distance, step, index):
        block = weight_piece(kind, source(distance), index)
        return seq_copy(
            block, block, wf_s.at[kind, distance, step], wf_r.at[kind, distance, step],
            (base + lax.rem(place + step, RING)) * 2 + half,
        )

    def core_copy(kind, distance):
        owner = source(distance)
        if kind == 1:
            block = cross_w.at[owner, :, :, own_lanes]
        else:
            block = out_w.at[kind // 2, owner, :, half]
        return seq_copy(
            block, block, wc_s.at[kind, distance], wc_r.at[kind, distance], other_core
        )

    def ring_steps(action):
        def step(i, carry):
            action(i + 1)
            return carry

        lax.fori_loop(0, RING - 1, step, 0)

    def fetch_weights(kind):
        for distance in range(1, parts):
            weight_copy(kind, distance).start()

    def pass_weights(kind):
        for distance in range(1, parts):
            weight_copy(kind, distance).wait_recv()
            ring_steps(lambda step: ring_copy(kind, distance, step, place).start())

    def swap_weights(kind):
        for distance in range(1, parts):
            ring_steps(
                lambda step: ring_copy(
                    kind, distance, step, lax.rem(place + RING - step, RING)
                ).wait_recv()
            )
            core_copy(kind, distance).start()

    def finish_weights(kind):
        for distance in range(1, parts):
            core_copy(kind, distance).wait_recv()

    def out_weight(layer, part):
        return out_w[layer, part].reshape(heads_width, part_width)

    def note_statistics(values, start, count):
        centre = jnp.sum(values, axis=1, keepdims=True) * (1.0 / part_width)
        offset = values - centre
        spread = jnp.sum(offset * offset, axis=1, keepdims=True)
        lane = lax.broadcasted_iota(jnp.int32, (count, 128), 1)
        cols[pl.ds(start, count), :] = jnp.where(lane == 0, centre, spread)

    def stat_copy(layer, distance):
        return fsdp_copy(
            stats.at[layer, me], stats.at[layer, me],
            stat_s.at[layer, distance], stat_r.at[layer, distance], distance,
        )

    def send_statistics(layer):
        stats[layer, me] = jnp.transpose(cols[...])[:8]
        for distance in range(1, parts):
            stat_copy(layer, distance).start()

    def finish_statistics(layer):
        for distance in range(1, parts):
            stat_copy(layer, distance).wait_recv()
        centre = jnp.zeros((1, rows), jnp.float32)
        for part in range(parts):
            centre = centre + stats[layer, part][0:1]
        centre = centre * (1.0 / parts)
        spread = jnp.zeros((1, rows), jnp.float32)
        for part in range(parts):
            shift = stats[layer, part][0:1] - centre
            spread = spread + stats[layer, part][1:2] * (1.0 / part_width) + shift * shift
        inverse = lax.rsqrt(spread * (1.0 / parts) + EPS)
        line = lax.broadcasted_iota(jnp.int32, (128, rows), 0)
        cols[...] = jnp.transpose(jnp.where(line == 0, centre, inverse))

    def chunk_rows(index):
        return pl.ds(pl.multiple_of(index * chunk, chunk), chunk)

    def block_rows(index):
        return pl.ds(pl.multiple_of(index * BLOCK, BLOCK), BLOCK)

    def h_copy(index, distance):
        block = normed.at[me, chunk_rows(index)]
        return fsdp_copy(
            block, block, h_s.at[distance, index], h_r.at[distance, index], distance
        )

    def normalised(layer, span):
        line = cols[span, :]
        shift = mods[layer, 0:1]
        gain = 1.0 + mods[layer, 1:2]
        values = (stream[span, :] - line[:, 0:1]) * line[:, 1:2] * gain + shift
        return values.astype(jnp.bfloat16)

    load_tokens().wait()

    def first_statistics(i, carry):
        start = pl.multiple_of(i * chunk, chunk)
        note_statistics(stream[pl.ds(start, chunk), :], start, chunk)
        return carry

    lax.fori_loop(0, chunks, first_statistics, 0)
    send_statistics(0)
    for kind in range(3):
        fetch_weights(kind)
    for layer in range(2):
        load_mod(layer).wait()
    load_time().start()
    load_out(0).start()
    load_out(1).start()
    finish_statistics(0)

    def space_send(index, carry):
        span = chunk_rows(index)
        normed[me, span, :] = normalised(0, span)
        for distance in range(1, parts):
            h_copy(index, distance).start()
        return carry

    lax.fori_loop(0, chunks, space_send, 0)
    for kind in range(3):
        pass_weights(kind)
    for kind in range(3):
        load_space(kind).wait()

    def space_depth(owner):
        return pl.ds(pl.multiple_of(owner * part_width, 128), part_width)

    def space_own(index, carry):
        span = block_rows(index)
        total[span, :] = jnp.dot(
            normed[me, span, :], space_w[space_depth(me), :], preferred_element_type=jnp.float32
        )
        return carry

    lax.fori_loop(0, query_blocks, space_own, 0)

    def kv_copy(index):
        block = keys_values.at[half, :, chunk_rows(index)]
        return seq_copy(block, block, kv_s.at[index], kv_r.at[index], other_core)

    def space_chunk(index, carry):
        span = chunk_rows(index)
        value = total[span, :]
        for distance in range(1, parts):
            h_copy(index, distance).wait_recv()
            other = source(distance)
            value = value + jnp.dot(
                normed[other, span, :], space_w[space_depth(other), :],
                preferred_element_type=jnp.float32,
            )
        value = value.astype(jnp.bfloat16)
        queries[span, :] = value[:, :heads_width]
        for kind in range(2):
            first = (kind + 1) * heads_width
            keys_values[half, kind, span, :] = value[:, first:first + heads_width]
        kv_copy(index).start()
        return carry

    lax.fori_loop(0, chunks, space_chunk, 0)
    swap_weights(0)

    def wait_keys(index, carry):
        kv_copy(index).wait_recv()
        return carry

    lax.fori_loop(0, chunks, wait_keys, 0)

    def att_space_copy(index, distance):
        block = att_space.at[me, block_rows(index)]
        return fsdp_copy(
            block, block, as_s.at[distance, index], as_r.at[distance, index], distance
        )

    def space_attention(index, carry):
        span = block_rows(index)
        bias = []
        for key_block in range(2 * query_blocks):
            kept = mask_ref[half * query_blocks + index, frame, key_block]
            bias.append(jnp.full((1, BLOCK), jnp.where(kept == 1, 0.0, -jnp.inf), jnp.float32))
        bias = jnp.concatenate(bias, axis=1)
        for head in range(local_heads):
            lanes = slice(head * HD, (head + 1) * HD)
            keys = keys_values[:, 0, :, lanes].reshape(2 * rows, HD)
            values = keys_values[:, 1, :, lanes].reshape(2 * rows, HD)
            scores = lax.dot_general(
                queries[span, lanes], keys, NT, preferred_element_type=jnp.float32
            )
            weights = softmax_rounded(scores * scale + bias)
            att_space[me, span, lanes] = jnp.dot(
                weights, values, preferred_element_type=jnp.float32
            ).astype(jnp.bfloat16)
        for distance in range(1, parts):
            att_space_copy(index, distance).start()
        return carry

    lax.fori_loop(0, query_blocks, space_attention, 0)
    load_out(0).wait()
    finish_weights(0)

    def space_project(index, carry):
        span = block_rows(index)
        for distance in range(1, parts):
            att_space_copy(index, distance).wait_recv()
        summed = jnp.zeros((BLOCK, part_width), jnp.float32)
        for part in range(parts):
            summed = summed + jnp.dot(
                att_space[part, span, :], out_weight(0, part), preferred_element_type=jnp.float32
            ).astype(jnp.bfloat16).astype(jnp.float32)
        values = stream[span, :] + mods[0, 2:3] * summed
        stream[span, :] = values
        note_statistics(values, pl.multiple_of(index * BLOCK, BLOCK), BLOCK)
        return carry

    lax.fori_loop(0, query_blocks, space_project, 0)

    send_statistics(1)
    swap_weights(1)
    load_time().wait()
    finish_statistics(1)
    finish_weights(1)

    def time_order(i):
        return lax.rem(frame // per_step + 1 + i, STEPS)

    def step_span(index):
        return pl.ds(pl.multiple_of(index * step_rows, step_rows), step_rows)

    def part_copy(index, distance):
        span = step_span(index)
        return fsdp_copy(
            part_sent.at[distance, span], part_got.at[distance, span],
            p_s.at[distance, index], p_r.at[distance, index], distance,
        )

    def kind_lanes(kind):
        return slice(kind * heads_width, (kind + 1) * heads_width)

    def time_send(i):
        index = time_order(i)
        span = step_span(index)
        values = normalised(1, span)
        h_time[span, :] = values
        for distance in range(1, parts):
            for kind in range(3):
                part_sent[distance, span, kind_lanes(kind)] = jnp.dot(
                    values, cross_w[peer(distance), kind], preferred_element_type=jnp.float32
                ).astype(jnp.bfloat16)
            part_copy(index, distance).start()
        for kind in range(3):
            total[span, kind_lanes(kind)] = jnp.dot(
                h_time[span, :], cross_w[me, kind], preferred_element_type=jnp.float32
            )

    def tq_copy(target):
        return seq_copy(
            sent_qkv.at[target], got_qkv.at[frame], tq_s.at[target], tq_r.at[frame],
            target * 2 + half,
        )

    def tq_arrival(origin):
        return seq_copy(
            sent_qkv.at[origin], got_qkv.at[origin], tq_s.at[origin], tq_r.at[origin],
            origin * 2 + half,
        )

    def time_pass(i):
        index = time_order(i)
        span = step_span(index)
        whole = total[span, :]
        for distance in range(1, parts):
            part_copy(index, distance).wait_recv()
            whole = whole + part_got[distance, span, :].astype(jnp.float32)
        whole = whole.reshape(per_step, piece, 3 * heads_width).astype(jnp.bfloat16)
        for n in range(per_step):
            target = index * per_step + n
            sent_qkv[target] = whole[n]

            @pl.when(target != frame)
            def _():
                tq_copy(target).start()

    time_send(0)

    def time_step(i, carry):
        time_send(i)
        time_pass(i - 1)
        return carry

    lax.fori_loop(1, STEPS, time_step, 0)
    time_pass(STEPS - 1)
    swap_weights(2)
    got_qkv[frame] = sent_qkv[frame]

    def others(action):
        def step(i, carry):
            action(lax.rem(frame + frames - 1 - i, frames))
            return carry

        lax.fori_loop(0, frames - 1, step, 0)

    others(lambda origin: tq_arrival(origin).wait_recv())

    def position(index):
        passed = jnp.zeros_like(index)
        for n in range(1, frames):
            passed = passed + jnp.where(index >= n * piece, piece, 0)
        return index - passed

    def flat(first):
        return got_qkv[:, :, first:first + HD].astype(jnp.float32).reshape(rows, HD).astype(jnp.bfloat16)

    column = position(lax.broadcasted_iota(jnp.int32, (1, rows), 1))
    for head in range(local_heads):
        first = head * HD
        head_queries = flat(first)
        head_keys = flat(heads_width + first)
        head_values = flat(2 * heads_width + first)
        for block in range(query_blocks):
            span = slice(block * BLOCK, (block + 1) * BLOCK)
            line = position(lax.broadcasted_iota(jnp.int32, (BLOCK, 1), 0) + block * BLOCK)
            scores = lax.dot_general(
                head_queries[span], head_keys, NT, preferred_element_type=jnp.float32
            ) * scale
            weights = softmax_rounded(jnp.where(line == column, scores, -jnp.inf))
            mixed[span, first:first + HD] = jnp.dot(
                weights, head_values, preferred_element_type=jnp.float32
            )
    sent_att[...] = mixed[...].reshape(frames, piece, heads_width).astype(jnp.bfloat16)
    att_time[me, frame] = sent_att[frame]

    def ta_copy(target):
        return seq_copy(
            sent_att.at[target], att_time.at[me, frame], ta_s.at[target], ta_r.at[frame],
            target * 2 + half,
        )

    def ta_arrival(origin):
        return seq_copy(
            sent_att.at[origin], att_time.at[me, origin], ta_s.at[origin], ta_r.at[origin],
            origin * 2 + half,
        )

    def send_att(i, carry):
        ta_copy(lax.rem(frame + 1 + i, frames)).start()
        return carry

    lax.fori_loop(0, frames - 1, send_att, 0)

    def att_time_copy(index, distance):
        block = att_time.at[me, index]
        return fsdp_copy(
            block, block, at_s.at[distance, index], at_r.at[distance, index], distance
        )

    def forward(index):
        for distance in range(1, parts):
            att_time_copy(index, distance).start()

    forward(frame)

    def relay(origin):
        ta_arrival(origin).wait_recv()
        forward(origin)

    others(relay)
    load_out(1).wait()
    finish_weights(2)

    def result_copy(index):
        span = chunk_rows(index)
        return pltpu.make_async_copy(stream.at[span], result_ref.at[0, span], out_sem.at[index])

    def time_project(i, carry):
        index = lax.rem(frame // per_chunk + chunks - i, chunks)
        span = chunk_rows(index)
        for n in range(per_chunk):
            for distance in range(1, parts):
                att_time_copy(index * per_chunk + n, distance).wait_recv()
        summed = jnp.zeros((chunk, part_width), jnp.float32)
        for part in range(parts):
            attended = att_time[part, pl.ds(index * per_chunk, per_chunk)].astype(jnp.float32)
            summed = summed + jnp.dot(
                attended.reshape(chunk, heads_width).astype(jnp.bfloat16), out_weight(1, part),
                preferred_element_type=jnp.float32,
            ).astype(jnp.bfloat16).astype(jnp.float32)
        stream[span, :] = stream[span, :] + mods[1, 2:3] * summed
        result_copy(index).start()
        return carry

    lax.fori_loop(0, chunks, time_project, 0)

    def drain(i, carry):
        kv_copy(i).wait_send()
        for distance in range(1, parts):
            h_copy(i, distance).wait_send()
        result_copy(i).wait()
        return carry

    lax.fori_loop(0, chunks, drain, 0)

    def drain_steps(i, carry):
        for distance in range(1, parts):
            part_copy(i, distance).wait_send()
        return carry

    lax.fori_loop(0, STEPS, drain_steps, 0)

    def drain_blocks(i, carry):
        for distance in range(1, parts):
            att_space_copy(i, distance).wait_send()
        return carry

    lax.fori_loop(0, query_blocks, drain_blocks, 0)

    def drain_pieces(i, carry):
        for distance in range(1, parts):
            att_time_copy(i, distance).wait_send()
        return carry

    lax.fori_loop(0, frames, drain_pieces, 0)

    def drain_other(target):
        tq_copy(target).wait_send()
        ta_copy(target).wait_send()

    others(drain_other)
    for distance in range(1, parts):
        for layer in range(2):
            stat_copy(layer, distance).wait_send()
        for kind in range(3):
            weight_copy(kind, distance).wait_send()
            core_copy(kind, distance).wait_send()
            ring_steps(lambda step: ring_copy(kind, distance, step, place).wait_send())


def on_device(tokens, block_mask, space_qkv, space_out, space_mod, time_qkv, time_out, time_mod):
    videos, rows, part_width = tokens.shape
    heads_width = space_qkv.shape[2]
    frames = lax.axis_size("seq") // 2
    parts = lax.axis_size("fsdp")
    piece = rows // frames
    chunk = piece if piece % 16 == 0 else 2 * piece
    chunks = rows // chunk
    blocks = rows // BLOCK
    width = part_width * parts
    bf16, f32 = jnp.bfloat16, jnp.float32
    dma = pltpu.SemaphoreType.DMA
    cut_rows = lambda weight: weight.reshape(RING, 2, heads_width // (2 * RING), width)
    hbm = pl.BlockSpec(memory_space=pl.ANY)
    scratch = [
        pltpu.VMEM((rows, part_width), f32),
        pltpu.VMEM((rows, 128), f32),
        pltpu.VMEM((rows, 3 * heads_width), f32),
        pltpu.VMEM((rows, heads_width), bf16),
        pltpu.VMEM((2, 2, rows, heads_width), bf16),
        pltpu.VMEM((rows, heads_width), f32),
        pltpu.VMEM((frames, piece, 3 * heads_width), bf16),
        pltpu.VMEM((frames, piece, 3 * heads_width), bf16),
        pltpu.VMEM((frames, piece, heads_width), bf16),
        pltpu.VMEM((width, 3 * heads_width), bf16),
        pltpu.VMEM((parts, 3, part_width, heads_width), bf16),
        pltpu.VMEM((2, parts, RING, 2, heads_width // (2 * RING), part_width), bf16),
        pltpu.VMEM((2, 3, part_width), f32),
        pltpu.VMEM((2, parts, 8, rows), f32),
        pltpu.VMEM((parts, rows, part_width), bf16),
        pltpu.VMEM((rows, part_width), bf16),
        pltpu.VMEM((parts, rows, 3 * heads_width), bf16),
        pltpu.VMEM((parts, rows, 3 * heads_width), bf16),
        pltpu.VMEM((parts, rows, heads_width), bf16),
        pltpu.VMEM((parts, frames, piece, heads_width), bf16),
        dma, dma((3,)), dma, dma((2,)), dma((2,)), dma((chunks,)),
        dma((2, parts)), dma((2, parts)),
        dma((parts, chunks)), dma((parts, chunks)),
        dma((parts, STEPS)), dma((parts, STEPS)),
        dma((chunks,)), dma((chunks,)),
        dma((parts, blocks)), dma((parts, blocks)),
        dma((parts, frames)), dma((parts, frames)),
        dma((3, parts)), dma((3, parts)),
        dma((3, parts, RING)), dma((3, parts, RING)),
        dma((3, parts)), dma((3, parts)),
        dma((frames,)), dma((frames,)),
        dma((frames,)), dma((frames,)),
    ]
    sizes = (frames, parts, rows, part_width, heads_width, chunk)
    return pl.pallas_call(
        functools.partial(sublayers, sizes),
        out_shape=jax.ShapeDtypeStruct(tokens.shape, f32),
        in_specs=[pl.BlockSpec(memory_space=pltpu.SMEM)] + [hbm] * 7,
        out_specs=hbm,
        scratch_shapes=scratch,
        compiler_params=pltpu.CompilerParams(
            collective_id=0, has_side_effects=True, vmem_limit_bytes=58 * 1024 * 1024
        ),
        cost_estimate=pl.CostEstimate(
            flops=4 * rows * width * 4 * heads_width, bytes_accessed=20 * 1024 * 1024,
            transcendentals=1024 * 1024,
        ),
    )(
        jnp.swapaxes(block_mask, 0, 1), tokens, jnp.swapaxes(space_qkv, 0, 1), cut_rows(space_out), space_mod,
        jnp.swapaxes(time_qkv, 0, 1), cut_rows(time_out), time_mod,
    )


def solution(mesh):
    placed = (
        P(None, "seq", "fsdp"),
        P(),
        P(None, None, "fsdp"),
        P("fsdp", None),
        P(),
        P(None, None, "fsdp"),
        P("fsdp", None),
        P(),
    )
    return jax.shard_map(
        on_device, mesh=mesh, in_specs=placed, out_specs=P(None, "seq", "fsdp"), check_vma=False
    )
```

profile of v0, /device:TPU:0, one launch (start us, length us, event | category | flops | bytes accessed | tf_op | source)
XLA Modules:
  0.0 93.1 jit_solution(11687737534450928930)
XLA Ops:
  0.0 89.9 %shard_map.82 = f32[1,384,1536]{2,1,0:T(8,128)} custom-call(s32[6,8,6]{2,1,0:T(8,128)} %bitcast.9, f32[1,384,1536]{2,1,0:T(8,128)} %tokens_ref.1, bf16[3,3072,256]{2,1,0:T(8,128)(2,1)} %bitcast.5, bf16[8,2,16,3072]{3,2,1,0:T(8,128)(2,1)} %bitcast.7, f32[3,3072]{1,0:T(4,128)} %space_mod_ref.1, bf16[3,3072,256]{2,1,0:T(8,128)(2,1)} %bitcast.6, ...), custom_call_target="tpu_custom_call" | custom-call | flops 4831838208 | bytes 20971520 | tf_op jit(solution)/shard_map/pallas_call | solution.py:633
  89.9 3.2 %copy.10 = f32[1,384,1536]{2,1,0:T(8,128)} copy(f32[1,384,1536]{2,1,0:T(8,128)} %shard_map.82) | data formatting | bytes 4718592
where the time goes:
time: 93.4 us; the launch traced here: 93.1 us
  Pallas kernels  89.9 us (96%)
  local copies, waits for them, and re-layouts  3.22 us (3%)
    pallas_call x1, Pallas kernels, on_device(): pl.pallas_call(functools.partial(sublayers, sizes), out_shape=jax.ShapeDt...  89.9 us
    unnamed x1, local copies, waits for them, and re-layouts  3.22 us

commit v1 on v0

--- a/solution.py
+++ b/solution.py
@@ -138,12 +138,22 @@
             wq_s.at[kind, distance], wq_r.at[kind, distance], distance,
         )
 
-    def ring_copy(kind, distance, step, index):
+    twin = place + 1 - 2 * lax.rem(place, 2)
+    half_ring = RING // 2
+
+    def place_copy(kind, distance, slot, index, target):
         block = weight_piece(kind, source(distance), index)
         return seq_copy(
-            block, block, wf_s.at[kind, distance, step], wf_r.at[kind, distance, step],
-            (base + lax.rem(place + step, RING)) * 2 + half,
-        )
+            block, block, wf_s.at[kind, distance, slot], wf_r.at[kind, distance, slot],
+            (base + target) * 2 + half,
+        )
+
+    def ring_copy(kind, distance, step, index):
+        return place_copy(kind, distance, step, index, lax.rem(place + 2 * step, RING))
+
+    def twin_copy(kind, distance, step, own):
+        index = lax.rem(own + RING - 2 * step, RING)
+        return place_copy(kind, distance, half_ring + step, index, twin)
 
     def core_copy(kind, distance):
         owner = source(distance)
@@ -155,13 +165,6 @@
             block, block, wc_s.at[kind, distance], wc_r.at[kind, distance], other_core
         )
 
-    def ring_steps(action):
-        def step(i, carry):
-            action(i + 1)
-            return carry
-
-        lax.fori_loop(0, RING - 1, step, 0)
-
     def fetch_weights(kind):
         for distance in range(1, parts):
             weight_copy(kind, distance).start()
@@ -169,15 +172,20 @@
     def pass_weights(kind):
         for distance in range(1, parts):
             weight_copy(kind, distance).wait_recv()
-            ring_steps(lambda step: ring_copy(kind, distance, step, place).start())
+            for step in range(1, half_ring):
+                ring_copy(kind, distance, step, place).start()
+            twin_copy(kind, distance, 0, place).start()
+
+    def relay_weights(kind):
+        for distance in range(1, parts):
+            for step in range(1, half_ring):
+                ring_copy(kind, distance, step, lax.rem(place + RING - 2 * step, RING)).wait_recv()
+                twin_copy(kind, distance, step, place).start()
 
     def swap_weights(kind):
         for distance in range(1, parts):
-            ring_steps(
-                lambda step: ring_copy(
-                    kind, distance, step, lax.rem(place + RING - step, RING)
-                ).wait_recv()
-            )
+            for step in range(half_ring):
+                twin_copy(kind, distance, step, twin).wait_recv()
             core_copy(kind, distance).start()
 
     def finish_weights(kind):
@@ -304,7 +312,11 @@
         kv_copy(index).start()
         return carry
 
-    lax.fori_loop(0, chunks, space_chunk, 0)
+    relay_weights(0)
+    lax.fori_loop(0, chunks // 2, space_chunk, 0)
+    relay_weights(1)
+    lax.fori_loop(chunks // 2, chunks, space_chunk, 0)
+    relay_weights(2)
     swap_weights(0)
 
     def wait_keys(index, carry):
@@ -436,7 +448,6 @@
 
     lax.fori_loop(1, STEPS, time_step, 0)
     time_pass(STEPS - 1)
-    swap_weights(2)
     got_qkv[frame] = sent_qkv[frame]
 
     def others(action):
@@ -505,6 +516,7 @@
             att_time_copy(index, distance).start()
 
     forward(frame)
+    swap_weights(2)
 
     def relay(origin):
         ta_arrival(origin).wait_recv()
@@ -578,7 +590,10 @@
         for kind in range(3):
             weight_copy(kind, distance).wait_send()
             core_copy(kind, distance).wait_send()
-            ring_steps(lambda step: ring_copy(kind, distance, step, place).wait_send())
+            for step in range(half_ring):
+                twin_copy(kind, distance, step, place).wait_send()
+                if step:
+                    ring_copy(kind, distance, step, place).wait_send()
 
 
 def on_device(tokens, block_mask, space_qkv, space_out, space_mod, time_qkv, time_out, time_mod):

time: 93.4 us -> 92.6 us (level)
  no operation moved by 1% of the time
where the time goes in v1:
time: 92.6 us; the launch traced here: 92.3 us
  Pallas kernels  89.1 us (96%)
  local copies, waits for them, and re-layouts  3.22 us (3%)
    pallas_call x1, Pallas kernels, on_device(): pl.pallas_call(functools.partial(sublayers, sizes), out_shape=jax.ShapeDt...  89.1 us
    unnamed x1, local copies, waits for them, and re-layouts  3.22 us

profile of v1, /device:TPU:0, one launch (start us, length us, event | category | flops | bytes accessed | tf_op | source)
XLA Modules:
  0.0 92.3 jit_solution(8100597893324727716)
XLA Ops:
  0.0 89.1 %shard_map.82 = f32[1,384,1536]{2,1,0:T(8,128)} custom-call(s32[6,8,6]{2,1,0:T(8,128)} %bitcast.9, f32[1,384,1536]{2,1,0:T(8,128)} %tokens_ref.1, bf16[3,3072,256]{2,1,0:T(8,128)(2,1)} %bitcast.5, bf16[8,2,16,3072]{3,2,1,0:T(8,128)(2,1)} %bitcast.7, f32[3,3072]{1,0:T(4,128)} %space_mod_ref.1, bf16[3,3072,256]{2,1,0:T(8,128)(2,1)} %bitcast.6, ...), custom_call_target="tpu_custom_call" | custom-call | flops 4831838208 | bytes 20971520 | tf_op jit(solution)/shard_map/pallas_call | solution.py:648
  89.1 3.2 %copy.10 = f32[1,384,1536]{2,1,0:T(8,128)} copy(f32[1,384,1536]{2,1,0:T(8,128)} %shard_map.82) | data formatting | bytes 4718592

commit v2 on v1

--- a/solution.py
+++ b/solution.py
@@ -27,7 +27,7 @@
     sizes,
     mask_ref, tokens_ref, space_qkv_ref, space_out_ref, space_mod_ref, time_qkv_ref, time_out_ref,
     time_mod_ref, result_ref,
-    stream, cols, total, queries, keys_values, mixed, sent_qkv, got_qkv, sent_att,
+    stream, cols, total, queries, keys_values, sent_qkv, got_qkv, sent_att,
     space_w, cross_w, out_w, mods, stats, normed, h_time, part_sent, part_got, att_space, att_time,
     in_sem, w_sem, x_sem, o_sem, m_sem, out_sem,
     stat_s, stat_r, h_s, h_r, p_s, p_r, kv_s, kv_r, as_s, as_r, at_s, at_r,
@@ -314,10 +314,9 @@
 
     relay_weights(0)
     lax.fori_loop(0, chunks // 2, space_chunk, 0)
+    swap_weights(0)
     relay_weights(1)
     lax.fori_loop(chunks // 2, chunks, space_chunk, 0)
-    relay_weights(2)
-    swap_weights(0)
 
     def wait_keys(index, carry):
         kv_copy(index).wait_recv()
@@ -354,6 +353,8 @@
         return carry
 
     lax.fori_loop(0, query_blocks, space_attention, 0)
+    relay_weights(2)
+    swap_weights(1)
     load_out(0).wait()
     finish_weights(0)
 
@@ -374,7 +375,6 @@
     lax.fori_loop(0, query_blocks, space_project, 0)
 
     send_statistics(1)
-    swap_weights(1)
     load_time().wait()
     finish_statistics(1)
     finish_weights(1)
@@ -468,25 +468,6 @@
     def flat(first):
         return got_qkv[:, :, first:first + HD].astype(jnp.float32).reshape(rows, HD).astype(jnp.bfloat16)
 
-    column = position(lax.broadcasted_iota(jnp.int32, (1, rows), 1))
-    for head in range(local_heads):
-        first = head * HD
-        head_queries = flat(first)
-        head_keys = flat(heads_width + first)
-        head_values = flat(2 * heads_width + first)
-        for block in range(query_blocks):
-            span = slice(block * BLOCK, (block + 1) * BLOCK)
-            line = position(lax.broadcasted_iota(jnp.int32, (BLOCK, 1), 0) + block * BLOCK)
-            scores = lax.dot_general(
-                head_queries[span], head_keys, NT, preferred_element_type=jnp.float32
-            ) * scale
-            weights = softmax_rounded(jnp.where(line == column, scores, -jnp.inf))
-            mixed[span, first:first + HD] = jnp.dot(
-                weights, head_values, preferred_element_type=jnp.float32
-            )
-    sent_att[...] = mixed[...].reshape(frames, piece, heads_width).astype(jnp.bfloat16)
-    att_time[me, frame] = sent_att[frame]
-
     def ta_copy(target):
         return seq_copy(
             sent_att.at[target], att_time.at[me, frame], ta_s.at[target], ta_r.at[frame],
@@ -499,12 +480,6 @@
             origin * 2 + half,
         )
 
-    def send_att(i, carry):
-        ta_copy(lax.rem(frame + 1 + i, frames)).start()
-        return carry
-
-    lax.fori_loop(0, frames - 1, send_att, 0)
-
     def att_time_copy(index, distance):
         block = att_time.at[me, index]
         return fsdp_copy(
@@ -515,7 +490,40 @@
         for distance in range(1, parts):
             att_time_copy(index, distance).start()
 
-    forward(frame)
+    column = position(lax.broadcasted_iota(jnp.int32, (1, rows), 1))
+    line = position(lax.broadcasted_iota(jnp.int32, (step_rows, 1), 0))
+    head_keys = [flat(heads_width + head * HD) for head in range(local_heads)]
+    head_values = [flat(2 * heads_width + head * HD) for head in range(local_heads)]
+
+    def time_attention(i, carry):
+        first = time_order(i) * per_step
+        mixed = []
+        for head in range(local_heads):
+            asked = got_qkv[pl.ds(first, per_step), :, head * HD:(head + 1) * HD]
+            asked = asked.astype(jnp.float32).reshape(step_rows, HD).astype(jnp.bfloat16)
+            scores = lax.dot_general(
+                asked, head_keys[head], NT, preferred_element_type=jnp.float32
+            ) * scale
+            weights = softmax_rounded(jnp.where(line == column, scores, -jnp.inf))
+            mixed.append(jnp.dot(weights, head_values[head], preferred_element_type=jnp.float32))
+        mixed = jnp.concatenate(mixed, axis=1).reshape(per_step, piece, heads_width)
+        mixed = mixed.astype(jnp.bfloat16)
+        for n in range(per_step):
+            target = first + n
+
+            @pl.when(target != frame)
+            def _():
+                sent_att[target] = mixed[n]
+                ta_copy(target).start()
+
+            @pl.when(target == frame)
+            def _():
+                att_time[me, frame] = mixed[n]
+                forward(frame)
+
+        return carry
+
+    lax.fori_loop(0, STEPS, time_attention, 0)
     swap_weights(2)
 
     def relay(origin):
@@ -602,7 +610,7 @@
     frames = lax.axis_size("seq") // 2
     parts = lax.axis_size("fsdp")
     piece = rows // frames
-    chunk = piece if piece % 16 == 0 else 2 * piece
+    chunk = rows // STEPS
     chunks = rows // chunk
     blocks = rows // BLOCK
     width = part_width * parts
@@ -616,7 +624,6 @@
         pltpu.VMEM((rows, 3 * heads_width), f32),
         pltpu.VMEM((rows, heads_width), bf16),
         pltpu.VMEM((2, 2, rows, heads_width), bf16),
-        pltpu.VMEM((rows, heads_width), f32),
         pltpu.VMEM((frames, piece, 3 * heads_width), bf16),
         pltpu.VMEM((frames, piece, 3 * heads_width), bf16),
         pltpu.VMEM((frames, piece, heads_width), bf16),

time: 92.6 us -> 90.9 us (0.982)
  Pallas kernels: 89.1 us -> 87.4 us
    pallas_call x1, Pallas kernels: 89.1 us -> 87.4 us  [on_device(): pl.pallas_call(functools.partial(sublayers, sizes), out_shape=jax.ShapeDt...]
where the time goes in v2:
time: 90.9 us; the launch traced here: 90.6 us
  Pallas kernels  87.4 us (96%)
  local copies, waits for them, and re-layouts  3.22 us (4%)
    pallas_call x1, Pallas kernels, on_device(): pl.pallas_call(functools.partial(sublayers, sizes), out_shape=jax.ShapeDt...  87.4 us
    unnamed x1, local copies, waits for them, and re-layouts  3.22 us

profile of v2, /device:TPU:0, one launch (start us, length us, event | category | flops | bytes accessed | tf_op | source)
XLA Modules:
  0.0 90.6 jit_solution(4139982439570912067)
XLA Ops:
  0.0 87.4 %shard_map.82 = f32[1,384,1536]{2,1,0:T(8,128)} custom-call(s32[6,8,6]{2,1,0:T(8,128)} %bitcast.9, f32[1,384,1536]{2,1,0:T(8,128)} %tokens_ref.1, bf16[3,3072,256]{2,1,0:T(8,128)(2,1)} %bitcast.5, bf16[8,2,16,3072]{3,2,1,0:T(8,128)(2,1)} %bitcast.7, f32[3,3072]{1,0:T(4,128)} %space_mod_ref.1, bf16[3,3072,256]{2,1,0:T(8,128)(2,1)} %bitcast.6, ...), custom_call_target="tpu_custom_call" | custom-call | flops 4831838208 | bytes 20971520 | tf_op jit(solution)/shard_map/pallas_call | solution.py:655
  87.4 3.2 %copy.10 = f32[1,384,1536]{2,1,0:T(8,128)} copy(f32[1,384,1536]{2,1,0:T(8,128)} %shard_map.82) | data formatting | bytes 4718592

commit v3 on v2

--- a/solution.py
+++ b/solution.py
@@ -256,7 +256,7 @@
 
     lax.fori_loop(0, chunks, first_statistics, 0)
     send_statistics(0)
-    for kind in range(3):
+    for kind in range(2):
         fetch_weights(kind)
     for layer in range(2):
         load_mod(layer).wait()
@@ -273,7 +273,8 @@
         return carry
 
     lax.fori_loop(0, chunks, space_send, 0)
-    for kind in range(3):
+    fetch_weights(2)
+    for kind in range(2):
         pass_weights(kind)
     for kind in range(3):
         load_space(kind).wait()
@@ -353,17 +354,18 @@
         return carry
 
     lax.fori_loop(0, query_blocks, space_attention, 0)
-    relay_weights(2)
+    pass_weights(2)
     swap_weights(1)
     load_out(0).wait()
     finish_weights(0)
 
     def space_project(index, carry):
         span = block_rows(index)
-        for distance in range(1, parts):
-            att_space_copy(index, distance).wait_recv()
         summed = jnp.zeros((BLOCK, part_width), jnp.float32)
-        for part in range(parts):
+        for distance in range(parts):
+            part = source(distance)
+            if distance:
+                att_space_copy(index, distance).wait_recv()
             summed = summed + jnp.dot(
                 att_space[part, span, :], out_weight(0, part), preferred_element_type=jnp.float32
             ).astype(jnp.bfloat16).astype(jnp.float32)
@@ -448,6 +450,7 @@
 
     lax.fori_loop(1, STEPS, time_step, 0)
     time_pass(STEPS - 1)
+    relay_weights(2)
     got_qkv[frame] = sent_qkv[frame]
 
     def others(action):

time: 90.9 us -> 91 us (level)
  no operation moved by 1% of the time
where the time goes in v3:
time: 91 us; the launch traced here: 90.8 us
  Pallas kernels  87.6 us (96%)
  local copies, waits for them, and re-layouts  3.22 us (4%)
    pallas_call x1, Pallas kernels, on_device(): pl.pallas_call(functools.partial(sublayers, sizes), out_shape=jax.ShapeDt...  87.6 us
    unnamed x1, local copies, waits for them, and re-layouts  3.22 us

profile of v3, /device:TPU:0, one launch (start us, length us, event | category | flops | bytes accessed | tf_op | source)
XLA Modules:
  0.0 90.8 jit_solution(2391379487896645758)
XLA Ops:
  0.0 87.6 %shard_map.82 = f32[1,384,1536]{2,1,0:T(8,128)} custom-call(s32[6,8,6]{2,1,0:T(8,128)} %bitcast.9, f32[1,384,1536]{2,1,0:T(8,128)} %tokens_ref.1, bf16[3,3072,256]{2,1,0:T(8,128)(2,1)} %bitcast.5, bf16[8,2,16,3072]{3,2,1,0:T(8,128)(2,1)} %bitcast.7, f32[3,3072]{1,0:T(4,128)} %space_mod_ref.1, bf16[3,3072,256]{2,1,0:T(8,128)(2,1)} %bitcast.6, ...), custom_call_target="tpu_custom_call" | custom-call | flops 4831838208 | bytes 20971520 | tf_op jit(solution)/shard_map/pallas_call | solution.py:658
  87.6 3.2 %copy.10 = f32[1,384,1536]{2,1,0:T(8,128)} copy(f32[1,384,1536]{2,1,0:T(8,128)} %shard_map.82) | data formatting | bytes 4718592

commit v4 on v3

--- a/solution.py
+++ b/solution.py
@@ -659,7 +659,7 @@
         functools.partial(sublayers, sizes),
         out_shape=jax.ShapeDtypeStruct(tokens.shape, f32),
         in_specs=[pl.BlockSpec(memory_space=pltpu.SMEM)] + [hbm] * 7,
-        out_specs=hbm,
+        out_specs=pl.BlockSpec(memory_space=pltpu.VMEM),
         scratch_shapes=scratch,
         compiler_params=pltpu.CompilerParams(
             collective_id=0, has_side_effects=True, vmem_limit_bytes=58 * 1024 * 1024

time: 91 us -> 92.2 us (1.013)
  Pallas kernels: 87.6 us -> 88.8 us
    pallas_call x1, Pallas kernels: 87.6 us -> 88.8 us  [on_device(): pl.pallas_call(functools.partial(sublayers, sizes), out_shape=jax.ShapeDt...]
where the time goes in v4:
time: 92.2 us; the launch traced here: 92 us
  Pallas kernels  88.8 us (96%)
  local copies, waits for them, and re-layouts  3.22 us (3%)
    pallas_call x1, Pallas kernels, on_device(): pl.pallas_call(functools.partial(sublayers, sizes), out_shape=jax.ShapeDt...  88.8 us
    unnamed x1, local copies, waits for them, and re-layouts  3.22 us

profile of v4, /device:TPU:0, one launch (start us, length us, event | category | flops | bytes accessed | tf_op | source)
XLA Modules:
  0.0 92.0 jit_solution(3899354757700078240)
XLA Ops:
  0.0 88.8 %shard_map.82 = f32[1,384,1536]{2,1,0:T(8,128)} custom-call(s32[6,8,6]{2,1,0:T(8,128)} %bitcast.9, f32[1,384,1536]{2,1,0:T(8,128)} %tokens_ref.1, bf16[3,3072,256]{2,1,0:T(8,128)(2,1)} %bitcast.5, bf16[8,2,16,3072]{3,2,1,0:T(8,128)(2,1)} %bitcast.7, f32[3,3072]{1,0:T(4,128)} %space_mod_ref.1, bf16[3,3072,256]{2,1,0:T(8,128)(2,1)} %bitcast.6, ...), custom_call_target="tpu_custom_call" | custom-call | flops 4831838208 | bytes 20971520 | tf_op jit(solution)/shard_map/pallas_call | solution.py:658
  88.8 3.2 %copy.10 = f32[1,384,1536]{2,1,0:T(8,128)} copy(f32[1,384,1536]{2,1,0:T(8,128)} %shard_map.82) | data formatting | bytes 4718592
